TPU v7x, 32 devices: a whole 2x2x4 slice. The times are simulated.
32 devices in a mesh: section: 8 (over z, x), expert: 4 (over y, core).
Axes of the slice: x: 2, y: 2, z: 4, core: 2. Of those that a mesh axis runs over, the one named last changes fastest.
Arguments:
- tokens: bfloat16 [8, 768, 1024], P('section', 'expert'), may hold values from -6 to 6
- out_grad: bfloat16 [8, 768, 1024], P('section', 'expert'), may hold values from -6 to 6
- expert_ids: int32 [8, 768, 2], P('section', 'expert'), may hold values from 0 to 3, all different within a row; in each aligned block of 192 rows (0 to 191, 192 to 383, ..., all dimensions but the last counted through in order) at most 192 rows name the same one
- gate_weights: float32 [8, 768, 2], P('section', 'expert'), may hold values from 0.2 to 1
- w_gate: bfloat16 [8, 4, 1024, 256], P('section', 'expert'), may hold values from -0.1875 to 0.1875
- w_up: bfloat16 [8, 4, 1024, 256], P('section', 'expert'), may hold values from -0.1875 to 0.1875
- w_down: bfloat16 [8, 4, 256, 1024], P('section', 'expert'), may hold values from -0.25 to 0.25
Outputs:
- token_grad: bfloat16 [8, 768, 1024], P('section', 'expert')
- grad_gate: bfloat16 [8, 4, 1024, 256], P('section', 'expert')
- grad_up: bfloat16 [8, 4, 1024, 256], P('section', 'expert')
- grad_down: bfloat16 [8, 4, 256, 1024], P('section', 'expert')
Inputs may be any that keep to these rules, and one draw needn't show every extreme that they name: `expert_ids`: each token names 2 different experts. Among the 192 tokens of one device (aligned blocks of rows of one section) no expert is named by more than 192 (token, choice) pairs, a bound that some block reaches.
All inputs are finite; a program needn't handle non-finite values.
Results may differ from a plain program's by a relative error of at most 0.009.
Values may be sent and summed in bfloat16 or wider, within the bound.
A program may use at most 64 MiB of HBM per device.

v0:
```python
import math

import jax
import jax.numpy as jnp
from jax import lax
from jax.sharding import PartitionSpec as P


def partner(value, axis, bit):
    mask = 2**bit
    pairs = [(source, source ^ mask) for source in range(lax.axis_size(axis))]
    return lax.ppermute(value, axis, pairs)


def make_slots(ids, gates, inputs, grads, cap, experts):
    tok, topk = ids.shape
    width = inputs.shape[1]
    count = tok * topk
    flat = ids.reshape(count)
    onehot = (flat[:, None] == jnp.arange(experts, dtype=jnp.int32)[None, :]).astype(jnp.int32)
    before = jnp.cumsum(onehot, axis=0) - onehot
    rank = jnp.sum(before * onehot, axis=1)
    slot = flat * cap + rank
    source = (
        jnp.full((experts * cap,), count, jnp.int32)
        .at[slot]
        .set(jnp.arange(count, dtype=jnp.int32))
    )
    token = source // topk
    padded_in = jnp.concatenate([inputs, jnp.zeros((1, width), inputs.dtype)], axis=0)
    scaled = (gates[:, :, None] * grads.astype(jnp.float32)[:, None, :]).astype(jnp.bfloat16)
    padded_grad = jnp.concatenate(
        [scaled.reshape(count, width), jnp.zeros((1, width), jnp.bfloat16)], axis=0
    )
    slot_in = padded_in[token].reshape(experts, cap, width)
    slot_grad = padded_grad[source].reshape(experts, cap, width)
    live = (source < count).reshape(experts, cap)
    return (slot_in, slot_grad, live, slot)


def unslot(slot_rows, slot, tok, topk):
    width = slot_rows.shape[-1]
    picked = slot_rows[slot].astype(jnp.float32).reshape(tok, topk, width)
    return jnp.sum(picked, axis=1).astype(jnp.bfloat16)


def expert_grads(rows_in, rows_grad, gate_w, up_w, down_w):
    contract_last = (((1,), (1,)), ((), ()))
    contract_rows = (((0,), (0,)), ((), ()))
    gate_pre = jnp.dot(rows_in, gate_w, preferred_element_type=jnp.float32)
    up_pre = jnp.dot(rows_in, up_w, preferred_element_type=jnp.float32)
    sigmoid_g = jax.nn.sigmoid(gate_pre)
    swish_val = gate_pre * sigmoid_g
    act = (swish_val * up_pre).astype(jnp.bfloat16)
    act_grad = lax.dot_general(rows_grad, down_w, contract_last, preferred_element_type=jnp.float32)
    gate_grad = (act_grad * up_pre * sigmoid_g * (1.0 + gate_pre * (1.0 - sigmoid_g))).astype(
        jnp.bfloat16
    )
    up_grad = (act_grad * swish_val).astype(jnp.bfloat16)
    pair_grad = lax.dot_general(
        gate_grad, gate_w, contract_last, preferred_element_type=jnp.float32
    )
    pair_grad = pair_grad + lax.dot_general(
        up_grad, up_w, contract_last, preferred_element_type=jnp.float32
    )
    grad_g = lax.dot_general(rows_in, gate_grad, contract_rows, preferred_element_type=jnp.float32)
    grad_u = lax.dot_general(rows_in, up_grad, contract_rows, preferred_element_type=jnp.float32)
    grad_d = lax.dot_general(act, rows_grad, contract_rows, preferred_element_type=jnp.float32)
    return (pair_grad, grad_g, grad_u, grad_d)


def run_expert(rows_in, rows_grad, gate_w, up_w, down_w):
    return expert_grads(rows_in, rows_grad, gate_w, up_w, down_w)


def per_device(tokens, out_grad, expert_ids, gate_weights, w_gate, w_up, w_down):
    inputs = tokens[0]
    grads = out_grad[0]
    ids = expert_ids[0]
    gates = gate_weights[0]
    tok, topk = ids.shape
    width = inputs.shape[1]
    experts = lax.axis_size("expert")
    cap = 2 * topk * tok // experts
    scale = 1.0 / math.sqrt(2 * topk * tok)
    pair_bit = lax.axis_size("section").bit_length() - 2
    slot_in, slot_grad, live, slot = make_slots(ids, gates, inputs, grads, cap, experts)
    recv_in, recv_grad, recv_live = (
        lax.all_to_all(slot_in, "expert", split_axis=0, concat_axis=0, tiled=True),
        lax.all_to_all(slot_grad, "expert", split_axis=0, concat_axis=0, tiled=True),
        lax.all_to_all(
            live.astype(jnp.bfloat16), "expert", split_axis=0, concat_axis=0, tiled=True
        ),
    )
    rows = experts * cap
    recv_in = recv_in.reshape(rows, width)
    recv_grad = recv_grad.reshape(rows, width)
    recv_live = recv_live.reshape(rows)
    own_gate = w_gate[0, 0]
    own_up = w_up[0, 0]
    own_down = w_down[0, 0]
    half = own_gate.shape[1]
    other_gate, other_up, other_down = partner((own_gate, own_up, own_down), "section", pair_bit)
    full_gate = jnp.concatenate([own_gate, other_gate], axis=1)
    full_up = jnp.concatenate([own_up, other_up], axis=1)
    full_down = jnp.concatenate([own_down, other_down], axis=0)
    pair_grad, grad_g, grad_u, grad_d = run_expert(
        recv_in, recv_grad, full_gate, full_up, full_down
    )
    peer_g, peer_u, peer_d = (
        partner(grad_g[:, half:].astype(jnp.bfloat16), "section", pair_bit).astype(jnp.float32),
        partner(grad_u[:, half:].astype(jnp.bfloat16), "section", pair_bit).astype(jnp.float32),
        partner(grad_d[half:, :].astype(jnp.bfloat16), "section", pair_bit).astype(jnp.float32),
    )
    mine_g = grad_g[:, :half] + peer_g
    mine_u = grad_u[:, :half] + peer_u
    mine_d = grad_d[:half, :] + peer_d
    back_slots = pair_grad.astype(jnp.bfloat16).reshape(experts, cap, width)
    home_slots = lax.all_to_all(back_slots, "expert", split_axis=0, concat_axis=0, tiled=True)
    token_grad = unslot(home_slots.reshape(rows, width), slot, tok, topk)
    out_g = (mine_g * scale).astype(jnp.bfloat16)
    out_u = (mine_u * scale).astype(jnp.bfloat16)
    out_d = (mine_d * scale).astype(jnp.bfloat16)
    return (token_grad[None], out_g[None, None], out_u[None, None], out_d[None, None])


def solution(mesh):
    in_specs = (
        P("section", "expert", None),
        P("section", "expert", None),
        P("section", "expert", None),
        P("section", "expert", None),
        P("section", "expert", None, None),
        P("section", "expert", None, None),
        P("section", "expert", None, None),
    )
    out_specs = (
        P("section", "expert", None),
        P("section", "expert", None, None),
        P("section", "expert", None, None),
        P("section", "expert", None, None),
    )
    return jax.shard_map(
        per_device, mesh=mesh, in_specs=in_specs, out_specs=out_specs, check_vma=False
    )
```

profile of v0, /device:TPU:0, one launch (start us, length us, event | category | flops | bytes accessed | tf_op | source)
XLA Modules:
  0.0 187.5 jit_solution(936301885651108846)
XLA Ops:
  2.4 1.2 reduce-window.6
  4.4 2.9 %scatter_custom_fusion = s32[768]{0:T(1024)S(1)} fusion(s32[384]{0:T(512)S(1)} %fusion.27, s32[384]{0:T(512)S(1)} %iota.11, s32[]{:T(128)} %constant.13.clone.1), kind=kCustom, calls=%fused_computation.59 | custom fusion | bytes 3076 | tf_op jit(solution)/shard_map/scatter | solution.py:27
  7.4 1.0 concatenate.17
  8.4 3.6 %gather_fusion.1 = bf16[768,1024]{1,0:T(8,128)(2,1)} fusion(bf16[193,1024]{1,0:T(8,128)(2,1)S(1)} %concatenate.17, s32[1024]{0:T(1024)S(1)} %get-tuple-element.8), kind=kCustom, calls=%fused_computation.1 | custom fusion | bytes 3148800 | tf_op jit(solution)/shard_map/gather | solution.py:35
  12.0 4.5 %all-to-all-start.1 = ((bf16[4,192,1024]{2,1,0:T(8,128)(2,1)}), bf16[4,192,1024]{2,1,0:T(8,128)(2,1)}, u32[]{:S(2)}, u32[]{:S(2)}) async-start(bf16[4,192,1024]{2,1,0:T(8,128)(2,1)} %bitcast.6), calls=%async_computation.1 | async-start | bytes 3145728 | tf_op jit(solution)/shard_map/all_to_all | solution.py:89
  17.1 1.1 mul.73
  18.7 3.6 %gather_fusion = bf16[768,1024]{1,0:T(8,128)(2,1)} fusion(bf16[385,1024]{1,0:T(8,128)(2,1)S(1)} %concatenate.15, s32[1024]{0:T(1024)S(1)} %get-tuple-element.9), kind=kCustom, calls=%fused_computation | custom fusion | bytes 3148800 | tf_op jit(solution)/shard_map/gather | solution.py:36
  22.3 15.0 %all-to-all-done.1 = bf16[4,192,1024]{2,1,0:T(8,128)(2,1)} async-done(((bf16[4,192,1024]{2,1,0:T(8,128)(2,1)}), bf16[4,192,1024]{2,1,0:T(8,128)(2,1)}, u32[]{:S(2)}, u32[]{:S(2)}) %all-to-all-start.1) | async-done | bytes 1572896 | tf_op jit(solution)/shard_map/all_to_all | solution.py:89
  37.3 3.7 %all-to-all-start = ((bf16[4,192,1024]{2,1,0:T(8,128)(2,1)}), bf16[4,192,1024]{2,1,0:T(8,128)(2,1)S(1)}, u32[]{:S(2)}, u32[]{:S(2)}) async-start(bf16[4,192,1024]{2,1,0:T(8,128)(2,1)} %bitcast.2), calls=%async_computation | async-start | bytes 3145728 | tf_op jit(solution)/shard_map/all_to_all | solution.py:90
  41.0 3.4 %collective-permute-start.2 = (bf16[1024,256]{1,0:T(8,128)(2,1)S(1)}, bf16[1024,256]{1,0:T(8,128)(2,1)S(1)}, u32[]{:S(2)}, u32[]{:S(2)}) collective-permute-start(bf16[1024,256]{1,0:T(8,128)(2,1)S(1)} %bitcast.55), channel_id=1, source_target_pairs={{0,16},{4,20},{8,24},{12,28},{16,0},{20,4},{24,8},{28,12},{1,17},{... | collective-permute-start | bytes 1572872 | tf_op jit(solution)/shard_map/ppermute | solution.py:12
  44.5 2.8 %collective-permute-start = (bf16[256,1024]{1,0:T(8,128)(2,1)S(1)}, bf16[256,1024]{1,0:T(8,128)(2,1)}, u32[]{:S(2)}, u32[]{:S(2)}) collective-permute-start(bf16[256,1024]{1,0:T(8,128)(2,1)S(1)} %bitcast.61), channel_id=1, source_target_pairs={{0,16},{4,20},{8,24},{12,28},{16,0},{20,4},{24,8},{28,12},{1,17},{... | collective-permute-start | bytes 1572872 | tf_op jit(solution)/shard_map/ppermute | solution.py:12
  47.4 43.5 %collective-permute-done.2 = bf16[1024,256]{1,0:T(8,128)(2,1)S(1)} collective-permute-done((bf16[1024,256]{1,0:T(8,128)(2,1)S(1)}, bf16[1024,256]{1,0:T(8,128)(2,1)S(1)}, u32[]{:S(2)}, u32[]{:S(2)}) %collective-permute-start.2) | collective-permute-done | bytes 524320 | tf_op jit(solution)/shard_map/ppermute | solution.py:12
  90.9 3.7 %fusion.12 = f32[768,512]{1,0:T(8,128)} fusion(bf16[768,1024]{1,0:T(8,128)(2,1)} %bitcast.7, bf16[1024,256]{1,0:T(8,128)(2,1)S(1)} %collective-permute-done.2, bf16[1024,256]{1,0:T(8,128)(2,1)S(1)} %bitcast.56), kind=kOutput, calls=%fused_computation.30 | convolution fusion | flops 807403520 | bytes 4194304 | tf_op jit(solution)/shard_map/dot_general | solution.py:50
  94.6 7.5 %collective-permute-done.1 = bf16[1024,256]{1,0:T(8,128)(2,1)S(1)} collective-permute-done((bf16[1024,256]{1,0:T(8,128)(2,1)S(1)}, bf16[1024,256]{1,0:T(8,128)(2,1)S(1)}, u32[]{:S(2)}, u32[]{:S(2)}) %collective-permute-start.1) | collective-permute-done | bytes 524320 | tf_op jit(solution)/shard_map/ppermute | solution.py:12
  102.9 3.6 %fusion.14 = f32[768,512]{1,0:T(8,128)} fusion(bf16[768,1024]{1,0:T(8,128)(2,1)} %bitcast.7, bf16[1024,256]{1,0:T(8,128)(2,1)S(1)} %collective-permute-done.1, bf16[1024,256]{1,0:T(8,128)(2,1)S(1)} %bitcast.53), kind=kOutput, calls=%fused_computation.32 | convolution fusion | flops 807403520 | bytes 4194304 | tf_op jit(solution)/shard_map/dot_general | solution.py:51
  106.6 3.1 %fusion.11 = f32[512,1024]{1,0:T(8,128)S(1)} fusion(bf16[768,1024]{1,0:T(8,128)(2,1)S(1)} %bitcast.50, f32[768,512]{1,0:T(8,128)} %fusion.14, f32[768,512]{1,0:T(8,128)} %fusion.12), kind=kOutput, calls=%fused_computation.29 | convolution fusion | flops 807665664 | bytes 6815744 | tf_op jit(solution)/shard_map/dot_general | solution.py:68
  111.2 2.0 %collective-permute-done = bf16[256,1024]{1,0:T(8,128)(2,1)} collective-permute-done((bf16[256,1024]{1,0:T(8,128)(2,1)S(1)}, bf16[256,1024]{1,0:T(8,128)(2,1)}, u32[]{:S(2)}, u32[]{:S(2)}) %collective-permute-start) | collective-permute-done | bytes 524320 | tf_op jit(solution)/shard_map/ppermute | solution.py:12
  113.2 2.5 %multiply_convert_fusion.2 = (bf16[768,512]{1,0:T(8,128)(2,1)S(1)}, bf16[768,512]{1,0:T(8,128)(2,1)S(1)}) fusion(f32[768,512]{1,0:T(8,128)S(1)} %copy-done.14, f32[768,512]{1,0:T(8,128)S(1)} %copy-done.15, bf16[768,1024]{1,0:T(8,128)(2,1)S(1)} %bitcast.51, bf16[256,1024]{1,0:T(8,128)(2,1)} %collective-permute-done, bf16[256,1024]{1,0:T(8,128)(2,1)S(1)} %bitcast.62), kind=kOutput, calls=%fused_computation.7 | convolution fusion | flops 812515328 | bytes 7340032 | tf_op jit(solution)/shard_map/dot_general | solution.py:55
  115.8 1.0 fusion.13
  117.0 2.2 %add_convert_fusion = bf16[768,1024]{1,0:T(8,128)(2,1)} fusion(f32[768,1024]{1,0:T(8,128)S(1)} %fusion.13, bf16[768,512]{1,0:T(8,128)(2,1)S(1)} %get-tuple-element.4, bf16[1024,256]{1,0:T(8,128)(2,1)S(1)} %copy-done.7, bf16[1024,256]{1,0:T(8,128)(2,1)S(1)} %bitcast.57), kind=kOutput, calls=%fused_computation.4 | convolution fusion | flops 808976384 | bytes 6553600 | tf_op jit(solution)/shard_map/dot_general | solution.py:60
  119.1 3.7 %all-to-all-start.2 = ((bf16[4,192,1024]{2,1,0:T(8,128)(2,1)}), bf16[4,192,1024]{2,1,0:T(8,128)(2,1)S(1)}, u32[]{:S(2)}, u32[]{:S(2)}) async-start(bf16[4,192,1024]{2,1,0:T(8,128)(2,1)} %bitcast.10), calls=%async_computation.2 | async-start | bytes 3145728 | tf_op jit(solution)/shard_map/all_to_all | solution.py:119
  122.9 2.4 %fusion.35 = f32[1024,512]{1,0:T(8,128)S(1)} fusion(bf16[768,1024]{1,0:T(8,128)(2,1)} %bitcast.7, bf16[768,512]{1,0:T(8,128)(2,1)S(1)} %get-tuple-element.5), kind=kOutput, calls=%fused_computation.70 | convolution fusion | flops 805306368 | bytes 4456448 | tf_op jit(solution)/shard_map/dot_general | solution.py:67
  125.9 2.6 %fusion.34 = f32[1024,512]{1,0:T(8,128)S(1)} fusion(bf16[768,1024]{1,0:T(8,128)(2,1)} %bitcast.7, bf16[768,512]{1,0:T(8,128)(2,1)S(1)} %get-tuple-element.4), kind=kOutput, calls=%fused_computation.69 | convolution fusion | flops 805306368 | bytes 4456448 | tf_op jit(solution)/shard_map/dot_general | solution.py:66
  128.5 2.6 %collective-permute-start.3 = (bf16[1024,256]{1,0:T(8,128)(2,1)S(1)}, bf16[1024,256]{1,0:T(8,128)(2,1)S(1)}, u32[]{:S(2)}, u32[]{:S(2)}) collective-permute-start(bf16[1024,256]{1,0:T(8,128)(2,1)S(1)} %slice.75), channel_id=1, source_target_pairs={{0,16},{4,20},{8,24},{12,28},{16,0},{20,4},{24,8},{28,12},{1,17},{... | collective-permute-start | bytes 1572872 | tf_op jit(solution)/shard_map/ppermute | solution.py:12
  131.1 6.7 %collective-permute-done.5 = bf16[256,1024]{1,0:T(8,128)(2,1)} collective-permute-done((bf16[256,1024]{1,0:T(8,128)(2,1)}, bf16[256,1024]{1,0:T(8,128)(2,1)}, u32[]{:S(2)}, u32[]{:S(2)}) %collective-permute-start.5) | collective-permute-done | bytes 524320 | tf_op jit(solution)/shard_map/ppermute | solution.py:12
  137.8 2.0 %fusion.17 = bf16[1,1,256,1024]{3,2,1,0:T(8,128)(2,1)} fusion(bf16[256,1024]{1,0:T(8,128)(2,1)} %collective-permute-done.5, f32[512,1024]{1,0:T(8,128)S(1)} %copy-done.1), kind=kLoop, calls=%fused_computation.35 | loop fusion | flops 1048576 | bytes 2097152 | tf_op jit(solution)/shard_map/broadcast_in_dim | solution.py:124
  139.8 31.6 %collective-permute-done.4 = bf16[1024,256]{1,0:T(8,128)(2,1)S(1)} collective-permute-done((bf16[1024,256]{1,0:T(8,128)(2,1)S(1)}, bf16[1024,256]{1,0:T(8,128)(2,1)S(1)}, u32[]{:S(2)}, u32[]{:S(2)}) %collective-permute-start.4) | collective-permute-done | bytes 524320 | tf_op jit(solution)/shard_map/ppermute | solution.py:12
  171.4 1.0 fusion.16
  172.4 8.9 %collective-permute-done.3 = bf16[1024,256]{1,0:T(8,128)(2,1)S(1)} collective-permute-done((bf16[1024,256]{1,0:T(8,128)(2,1)S(1)}, bf16[1024,256]{1,0:T(8,128)(2,1)S(1)}, u32[]{:S(2)}, u32[]{:S(2)}) %collective-permute-start.3) | collective-permute-done | bytes 524320 | tf_op jit(solution)/shard_map/ppermute | solution.py:12
  181.3 1.0 fusion.15
  182.3 2.1 %gather_fusion.2 = bf16[384,1024]{1,0:T(8,128)(2,1)S(1)} fusion(bf16[768,1024]{1,0:T(8,128)(2,1)S(1)} %bitcast.49, s32[1024]{0:T(1024)S(1)} %pad_clamp_fusion), kind=kCustom, calls=%fused_computation.2 | custom fusion | bytes 1574400 | tf_op jit(solution)/shard_map/gather | solution.py:43
  184.6 2.8 %reduce = bf16[192,1024]{1,0:T(8,128)(2,1)} reduce(bf16[192,2,1024]{2,1,0:T(2,128)(2,1)S(1)} %convert_element_type.82, bf16[]{:T(256)} %constant.12.clone.1), dimensions={1}, to_apply=%region_4.5.clone | reduce | flops 196608 | bytes 1179650 | tf_op jit(solution)/shard_map/reduce_sum | solution.py:44
  (63 shorter events, 7.2 us)
Async XLA Ops:
  12.0 4.5 %copy-start.10 = (bf16[1,192,1024]{2,1,0:T(8,128)(2,1)S(1)}, bf16[1,192,1024]{2,1,0:T(8,128)(2,1)}, u32[]{:S(2)}) copy-start(bf16[1,192,1024]{2,1,0:T(8,128)(2,1)} %param.8) | copy-start | bytes 1179652
  12.0 25.3 %all-to-all-start.1 = ((bf16[4,192,1024]{2,1,0:T(8,128)(2,1)}), bf16[4,192,1024]{2,1,0:T(8,128)(2,1)}, u32[]{:S(2)}, u32[]{:S(2)}) async-start(bf16[4,192,1024]{2,1,0:T(8,128)(2,1)} %bitcast.6), calls=%async_computation.1 | async-start | bytes 3145728 | tf_op jit(solution)/shard_map/all_to_all | solution.py:89
  17.1 1.1 copy-start.11
  37.3 3.7 %copy-start.4 = (bf16[1,1,1024,256]{3,2,1,0:T(8,128)(2,1)S(1)}, bf16[1,1,1024,256]{3,2,1,0:T(8,128)(2,1)}, u32[]{:S(2)}) copy-start(bf16[1,1,1024,256]{3,2,1,0:T(8,128)(2,1)} %param.11) | copy-start | bytes 1572868
  37.3 7.2 %copy-start.2 = (bf16[1,1,1024,256]{3,2,1,0:T(8,128)(2,1)S(1)}, bf16[1,1,1024,256]{3,2,1,0:T(8,128)(2,1)}, u32[]{:S(2)}) copy-start(bf16[1,1,1024,256]{3,2,1,0:T(8,128)(2,1)} %param.12) | copy-start | bytes 1572868
  37.3 7.3 %copy-start.12 = (bf16[1,1,256,1024]{3,2,1,0:T(8,128)(2,1)S(1)}, bf16[1,1,256,1024]{3,2,1,0:T(8,128)(2,1)}, u32[]{:S(2)}) copy-start(bf16[1,1,256,1024]{3,2,1,0:T(8,128)(2,1)} %param.13) | copy-start | bytes 1572868
  37.3 69.3 %all-to-all-start = ((bf16[4,192,1024]{2,1,0:T(8,128)(2,1)}), bf16[4,192,1024]{2,1,0:T(8,128)(2,1)S(1)}, u32[]{:S(2)}, u32[]{:S(2)}) async-start(bf16[4,192,1024]{2,1,0:T(8,128)(2,1)} %bitcast.2), calls=%async_computation | async-start | bytes 3145728 | tf_op jit(solution)/shard_map/all_to_all | solution.py:90
  41.0 49.9 %collective-permute-start.2 = (bf16[1024,256]{1,0:T(8,128)(2,1)S(1)}, bf16[1024,256]{1,0:T(8,128)(2,1)S(1)}, u32[]{:S(2)}, u32[]{:S(2)}) collective-permute-start(bf16[1024,256]{1,0:T(8,128)(2,1)S(1)} %bitcast.55), channel_id=1, source_target_pairs={{0,16},{4,20},{8,24},{12,28},{16,0},{20,4},{24,8},{28,12},{1,17},{... | collective-permute-start | bytes 1572872 | tf_op jit(solution)/shard_map/ppermute | solution.py:12
  44.4 57.7 %collective-permute-start.1 = (bf16[1024,256]{1,0:T(8,128)(2,1)S(1)}, bf16[1024,256]{1,0:T(8,128)(2,1)S(1)}, u32[]{:S(2)}, u32[]{:S(2)}) collective-permute-start(bf16[1024,256]{1,0:T(8,128)(2,1)S(1)} %bitcast.52), channel_id=1, source_target_pairs={{0,16},{4,20},{8,24},{12,28},{16,0},{20,4},{24,8},{28,12},{1,17},{... | collective-permute-start | bytes 1572872 | tf_op jit(solution)/shard_map/ppermute | solution.py:12
  44.5 68.7 %collective-permute-start = (bf16[256,1024]{1,0:T(8,128)(2,1)S(1)}, bf16[256,1024]{1,0:T(8,128)(2,1)}, u32[]{:S(2)}, u32[]{:S(2)}) collective-permute-start(bf16[256,1024]{1,0:T(8,128)(2,1)S(1)} %bitcast.61), channel_id=1, source_target_pairs={{0,16},{4,20},{8,24},{12,28},{16,0},{20,4},{24,8},{28,12},{1,17},{... | collective-permute-start | bytes 1572872 | tf_op jit(solution)/shard_map/ppermute | solution.py:12
  90.9 3.7 %copy-start.6 = (bf16[1024,256]{1,0:T(8,128)(2,1)}, bf16[1024,256]{1,0:T(8,128)(2,1)S(1)}, u32[]{:S(2)}) copy-start(bf16[1024,256]{1,0:T(8,128)(2,1)S(1)} %collective-permute-done.2) | copy-start | bytes 1572868
  102.2 0.8 copy-start.8
  106.5 6.7 %copy-start.13 = (bf16[1,1,256,1024]{3,2,1,0:T(8,128)(2,1)S(1)}, bf16[1,1,256,1024]{3,2,1,0:T(8,128)(2,1)}, u32[]{:S(2)}) copy-start(bf16[1,1,256,1024]{3,2,1,0:T(8,128)(2,1)} %param.13) | copy-start | bytes 1572868
  106.5 6.7 %copy-start.14 = (f32[768,512]{1,0:T(8,128)S(1)}, f32[768,512]{1,0:T(8,128)}, u32[]{:S(2)}) copy-start(f32[768,512]{1,0:T(8,128)} %fusion.12) | copy-start | bytes 4718596
  106.5 6.7 %copy-start.15 = (f32[768,512]{1,0:T(8,128)S(1)}, f32[768,512]{1,0:T(8,128)}, u32[]{:S(2)}) copy-start(f32[768,512]{1,0:T(8,128)} %fusion.14) | copy-start | bytes 4718596
  109.7 1.5 copy-start
  110.6 5.1 %copy-start.3 = (bf16[1,1,1024,256]{3,2,1,0:T(8,128)(2,1)S(1)}, bf16[1,1,1024,256]{3,2,1,0:T(8,128)(2,1)}, u32[]{:S(2)}) copy-start(bf16[1,1,1024,256]{3,2,1,0:T(8,128)(2,1)} %param.12) | copy-start | bytes 1572868
  110.6 5.1 %copy-start.9 = (bf16[1024,256]{1,0:T(8,128)(2,1)S(1)}, bf16[1024,256]{1,0:T(8,128)(2,1)}, u32[]{:S(2)}) copy-start(bf16[1024,256]{1,0:T(8,128)(2,1)} %copy-done.8) | copy-start | bytes 1572868
  110.6 27.1 %collective-permute-start.5 = (bf16[256,1024]{1,0:T(8,128)(2,1)}, bf16[256,1024]{1,0:T(8,128)(2,1)}, u32[]{:S(2)}, u32[]{:S(2)}) collective-permute-start(bf16[256,1024]{1,0:T(8,128)(2,1)} %slice.73), channel_id=1, source_target_pairs={{0,16},{4,20},{8,24},{12,28},{16,0},{20,4},{24,8},{28,12},{1,17},{... | collective-permute-start | bytes 1572872 | tf_op jit(solution)/shard_map/ppermute | solution.py:12
  115.8 1.0 copy-start.5
  115.8 1.2 copy-start.7
  119.1 63.1 %all-to-all-start.2 = ((bf16[4,192,1024]{2,1,0:T(8,128)(2,1)}), bf16[4,192,1024]{2,1,0:T(8,128)(2,1)S(1)}, u32[]{:S(2)}, u32[]{:S(2)}) async-start(bf16[4,192,1024]{2,1,0:T(8,128)(2,1)} %bitcast.10), calls=%async_computation.2 | async-start | bytes 3145728 | tf_op jit(solution)/shard_map/all_to_all | solution.py:119
  125.4 46.0 %collective-permute-start.4 = (bf16[1024,256]{1,0:T(8,128)(2,1)S(1)}, bf16[1024,256]{1,0:T(8,128)(2,1)S(1)}, u32[]{:S(2)}, u32[]{:S(2)}) collective-permute-start(bf16[1024,256]{1,0:T(8,128)(2,1)S(1)} %slice.74), channel_id=1, source_target_pairs={{0,16},{4,20},{8,24},{12,28},{16,0},{20,4},{24,8},{28,12},{1,17},{... | collective-permute-start | bytes 1572872 | tf_op jit(solution)/shard_map/ppermute | solution.py:12
  125.8 11.9 %copy-start.1 = (f32[512,1024]{1,0:T(8,128)S(1)}, f32[512,1024]{1,0:T(8,128)}, u32[]{:S(2)}) copy-start(f32[512,1024]{1,0:T(8,128)} %copy-done) | copy-start | bytes 6291460
  128.5 52.8 %collective-permute-start.3 = (bf16[1024,256]{1,0:T(8,128)(2,1)S(1)}, bf16[1024,256]{1,0:T(8,128)(2,1)S(1)}, u32[]{:S(2)}, u32[]{:S(2)}) collective-permute-start(bf16[1024,256]{1,0:T(8,128)(2,1)S(1)} %slice.75), channel_id=1, source_target_pairs={{0,16},{4,20},{8,24},{12,28},{16,0},{20,4},{24,8},{28,12},{1,17},{... | collective-permute-start | bytes 1572872 | tf_op jit(solution)/shard_map/ppermute | solution.py:12
where the time goes:
time: 188 us; the launch traced here: 187 us
  waiting for transfers between devices  115 us (61%)
  starting transfers between devices  21.3 us (11%)
  matrix products  21.1 us (11%)
  local copies, waits for them, and re-layouts  19.6 us (10%)
  other arithmetic  9.22 us (5%)
    ppermute x6, waiting for transfers between devices, partner(): return lax.ppermute(value, axis, pairs)  100 us
    all_to_all x1, waiting for transfers between devices, per_device(): lax.all_to_all(slot_in, 'expert', split_axis=0, concat_axis=0, tiled=True)  15 us
    ppermute x6, starting transfers between devices, partner(): return lax.ppermute(value, axis, pairs)  9.43 us
    all_to_all x1, starting transfers between devices, per_device(): lax.all_to_all(slot_in, 'expert', split_axis=0, concat_axis=0, tiled=True)  4.48 us
  transfers between devices with their start and end apart: 9, of which 7 were waited for; matrix products, arithmetic and copies ran while one was open for 17% of the time, Pallas kernels for 0%

commit v1 on v0

--- a/solution.py
+++ b/solution.py
@@ -1,9 +1,16 @@
+import functools
 import math
 
 import jax
 import jax.numpy as jnp
 from jax import lax
+from jax.experimental import pallas as pl
+from jax.experimental.pallas import tpu as pltpu
 from jax.sharding import PartitionSpec as P
+
+MESH = pl.DeviceIdType.MESH
+CHUNKS = 2
+SLOTS = 4
 
 
 def partner(value, axis, bit):
@@ -17,9 +24,9 @@
     width = inputs.shape[1]
     count = tok * topk
     flat = ids.reshape(count)
-    onehot = (flat[:, None] == jnp.arange(experts, dtype=jnp.int32)[None, :]).astype(jnp.int32)
-    before = jnp.cumsum(onehot, axis=0) - onehot
-    rank = jnp.sum(before * onehot, axis=1)
+    place = jnp.arange(count, dtype=jnp.int32)
+    earlier = (flat[:, None] == flat[None, :]) & (place[None, :] < place[:, None])
+    rank = jnp.sum(earlier.astype(jnp.int32), axis=1)
     slot = flat * cap + rank
     source = (
         jnp.full((experts * cap,), count, jnp.int32)
@@ -124,6 +131,249 @@
     return (token_grad[None], out_g[None, None], out_u[None, None], out_d[None, None])
 
 
+def gathered_kernel(
+    sections, scale, x_hbm, dy_hbm, gates_hbm, wg_hbm, wu_hbm, wd_hbm,
+    tok_out, g_out, u_out, d_out,
+    rows, gates, w_gu, w_d, hidden, acts, part_send, part_recv, part_own,
+    y_send, y_recv, z_send, z_recv, send_sem, recv_sem, local_sem,
+):
+    chunks, tr, width = rows.shape[1], rows.shape[4], rows.shape[5]
+    half = w_d.shape[0]
+    s, e = lax.axis_index("section"), lax.axis_index("expert")
+    mirror = (lax.rem(s + sections // 2, sections), e)
+    y_peer = (s, lax.rem(e + 2, 4))
+    core_peer = (s, e + 1 - 2 * lax.rem(e, 2))
+
+    local = []
+
+    def bring(src, dst):
+        copy = pltpu.make_async_copy(src, dst, local_sem.at[len(local)])
+        copy.start()
+        local.append(copy)
+
+    for k in range(chunks):
+        bring(x_hbm.at[pl.ds(k * tr, tr), :], rows.at[0, k, 0, 0])
+        bring(dy_hbm.at[pl.ds(k * tr, tr), :], rows.at[0, k, 1, 0])
+    bring(gates_hbm, gates.at[0, 0])
+    own_copies = len(local)
+    bring(wg_hbm, w_gu.at[:, pl.ds(0, half)])
+    bring(wu_hbm, w_gu.at[:, pl.ds(half, half)])
+    bring(wd_hbm, w_d)
+
+    barrier = pltpu.get_barrier_semaphore()
+    for peer in (mirror, y_peer, core_peer):
+        pl.semaphore_signal(barrier, inc=1, device_id=peer, device_id_type=MESH)
+    pl.semaphore_wait(barrier, 3)
+
+    sent = []
+
+    def send(src, dst, peer):
+        n = len(sent)
+        copy = pltpu.make_async_remote_copy(
+            src_ref=src, dst_ref=dst, send_sem=send_sem.at[n], recv_sem=recv_sem.at[n],
+            device_id=peer, device_id_type=MESH,
+        )
+        copy.start()
+        sent.append(copy)
+        return copy
+
+    def send_block(side, k, slot, to_side, to_slot, peer):
+        out = [send(rows.at[side, k, :, slot], rows.at[to_side, k, :, to_slot], peer)]
+        if k == 0:
+            out.append(send(gates.at[side, slot], gates.at[to_side, to_slot], peer))
+        return out
+
+    def arrived(copies):
+        for copy in copies:
+            copy.wait_recv()
+
+    for copy in local[:own_copies]:
+        copy.wait()
+    by_z, by_y, by_core = {}, {}, {}
+    for k in range(chunks):
+        by_z[k] = send_block(0, k, 0, 1, 0, mirror)
+        by_y[0, k] = send_block(0, k, 0, 0, 2, y_peer)
+        by_core[0, k] = send_block(0, k, 0, 0, 1, core_peer)
+
+    def from_y(side, k):
+        arrived(by_y[side, k])
+        by_core[side, k] += send_block(side, k, 2, side, 3, core_peer)
+
+    def from_z(k):
+        arrived(by_z[k])
+        by_y[1, k] = send_block(1, k, 0, 1, 2, y_peer)
+        by_core[1, k] = send_block(1, k, 0, 1, 1, core_peer)
+
+    lanes = lax.broadcasted_iota(jnp.int32, (tr, gates.shape[2]), 1)
+    contract_last = (((1,), (1,)), ((), ()))
+    by_part, by_y_part, by_z_part = {}, {}, {}
+
+    def stage(side, k):
+        arrived(by_core[side, k])
+        x = rows[side, k, 0].reshape(SLOTS * tr, width)
+        dy = rows[side, k, 1].reshape(SLOTS * tr, width)
+        columns = []
+        for slot in range(SLOTS):
+            turned = jnp.transpose(gates[side, slot])[k * tr : (k + 1) * tr, :]
+            columns.append(
+                jnp.sum(jnp.where(lanes == e, turned, 0.0), axis=1, keepdims=True)
+            )
+        weight = jnp.concatenate(columns, axis=0)
+        pre = jnp.dot(x, w_gu[...], preferred_element_type=jnp.float32)
+        act_grad = weight * lax.dot_general(
+            dy, w_d[...], contract_last, preferred_element_type=jnp.float32
+        )
+        gate_pre, up_pre = pre[:, :half], pre[:, half:]
+        sigmoid_g = jax.nn.sigmoid(gate_pre)
+        swish_val = gate_pre * sigmoid_g
+        acts[side, k] = (swish_val * up_pre * weight).astype(jnp.bfloat16)
+        hidden[side, k, :, :half] = (
+            act_grad * up_pre * sigmoid_g * (1.0 + gate_pre * (1.0 - sigmoid_g))
+        ).astype(jnp.bfloat16)
+        hidden[side, k, :, half:] = (act_grad * swish_val).astype(jnp.bfloat16)
+        part = lax.dot_general(
+            hidden[side, k], w_gu[...], contract_last, preferred_element_type=jnp.float32
+        )
+        part_send[side, k, 0] = part[tr : 2 * tr].astype(jnp.bfloat16)
+        part_send[side, k, 1] = part[3 * tr :].astype(jnp.bfloat16)
+        by_part[side, k] = send(part_send.at[side, k], part_recv.at[side, k], core_peer)
+        part_own[side, k, 0] = part[:tr]
+        part_own[side, k, 1] = part[2 * tr : 3 * tr]
+
+    def add_core(side, k):
+        by_part[side, k].wait_recv()
+        y_send[side, k] = (
+            part_own[side, k, 1] + part_recv[side, k, 1].astype(jnp.float32)
+        ).astype(jnp.bfloat16)
+        by_y_part[side, k] = send(y_send.at[side, k], y_recv.at[side, k], y_peer)
+        part_own[side, k, 0] += part_recv[side, k, 0].astype(jnp.float32)
+
+    def add_y(side, k):
+        by_y_part[side, k].wait_recv()
+        total = part_own[side, k, 0] + y_recv[side, k].astype(jnp.float32)
+        if side:
+            z_send[k] = total.astype(jnp.bfloat16)
+            by_z_part[k] = send(z_send.at[k], z_recv.at[k], mirror)
+        else:
+            part_own[side, k, 0] = total
+
+    def add_z(k):
+        by_z_part[k].wait_recv()
+        tok_out[pl.ds(k * tr, tr), :] = (
+            part_own[0, k, 0] + z_recv[k].astype(jnp.float32)
+        ).astype(jnp.bfloat16)
+
+    tile = half
+    contract_rows = (((0,), (0,)), ((), ()))
+
+    def weight_grads(first, last):
+        @pl.loop(first, last)
+        def _(i):
+            span = pl.ds(pl.multiple_of(i * tile, tile), tile)
+            total_gu = jnp.zeros((tile, 2 * half), jnp.float32)
+            total_d = jnp.zeros((half, tile), jnp.float32)
+            for side in range(2):
+                for k in range(chunks):
+                    x = rows[side, k, 0, :, :, span].reshape(SLOTS * tr, tile)
+                    dy = rows[side, k, 1, :, :, span].reshape(SLOTS * tr, tile)
+                    total_gu += lax.dot_general(
+                        x, hidden[side, k], contract_rows, preferred_element_type=jnp.float32
+                    )
+                    total_d += lax.dot_general(
+                        acts[side, k], dy, contract_rows, preferred_element_type=jnp.float32
+                    )
+            total_gu = (total_gu * scale).astype(jnp.bfloat16)
+            g_out[span, :] = total_gu[:, :half]
+            u_out[span, :] = total_gu[:, half:]
+            d_out[:, span] = (total_d * scale).astype(jnp.bfloat16)
+
+    from_y(0, 0)
+    for copy in local[own_copies:]:
+        copy.wait()
+    stage(0, 0)
+    from_y(0, 1)
+    from_z(0)
+    add_core(0, 0)
+    stage(0, 1)
+    from_y(1, 0)
+    add_core(0, 1)
+    add_y(0, 0)
+    stage(1, 0)
+    from_z(1)
+    add_core(1, 0)
+    add_y(0, 1)
+    add_y(1, 0)
+    from_y(1, 1)
+    stage(1, 1)
+    tiles = width // tile
+    weight_grads(0, tiles // 4)
+    add_core(1, 1)
+    weight_grads(tiles // 4, tiles // 2)
+    add_y(1, 1)
+    weight_grads(tiles // 2, tiles)
+    add_z(0)
+    add_z(1)
+    for copy in sent:
+        copy.wait_send()
+
+
+def gathered(tokens, out_grad, expert_ids, gate_weights, w_gate, w_up, w_down):
+    tok, width = tokens.shape[1:]
+    topk = expert_ids.shape[2]
+    half = w_gate.shape[3]
+    sections = lax.axis_size("section")
+    scale = 1.0 / math.sqrt(2 * topk * tok)
+    tr = tok // CHUNKS
+    names = jnp.arange(8, dtype=jnp.int32)[:, None, None]
+    dense = jnp.sum(
+        jnp.where(expert_ids[0][None] == names, gate_weights[0][None], 0.0), axis=2
+    )
+    lanes = -(-tok // 128) * 128
+    dense = jnp.pad(dense, ((0, 0), (0, lanes - tok)))
+    bf16, f32 = jnp.bfloat16, jnp.float32
+    any_spec = pl.BlockSpec(memory_space=pl.ANY)
+    vmem_spec = pl.BlockSpec(memory_space=pltpu.VMEM)
+    copies = 12 * CHUNKS + 7
+    macs = 8 * 8 * tok * width * half
+    outs = pl.pallas_call(
+        functools.partial(gathered_kernel, sections, scale),
+        out_shape=(
+            jax.ShapeDtypeStruct((tok, width), bf16),
+            jax.ShapeDtypeStruct((width, half), bf16),
+            jax.ShapeDtypeStruct((width, half), bf16),
+            jax.ShapeDtypeStruct((half, width), bf16),
+        ),
+        in_specs=[any_spec] * 6,
+        out_specs=(vmem_spec,) * 4,
+        scratch_shapes=[
+            pltpu.VMEM((2, CHUNKS, 2, SLOTS, tr, width), bf16),
+            pltpu.VMEM((2, SLOTS, 8, lanes), f32),
+            pltpu.VMEM((width, 2 * half), bf16),
+            pltpu.VMEM((half, width), bf16),
+            pltpu.VMEM((2, CHUNKS, SLOTS * tr, 2 * half), bf16),
+            pltpu.VMEM((2, CHUNKS, SLOTS * tr, half), bf16),
+            pltpu.VMEM((2, CHUNKS, 2, tr, width), bf16),
+            pltpu.VMEM((2, CHUNKS, 2, tr, width), bf16),
+            pltpu.VMEM((2, CHUNKS, 2, tr, width), f32),
+            pltpu.VMEM((2, CHUNKS, tr, width), bf16),
+            pltpu.VMEM((2, CHUNKS, tr, width), bf16),
+            pltpu.VMEM((CHUNKS, tr, width), bf16),
+            pltpu.VMEM((CHUNKS, tr, width), bf16),
+            pltpu.SemaphoreType.DMA((copies,)),
+            pltpu.SemaphoreType.DMA((copies,)),
+            pltpu.SemaphoreType.DMA((2 * CHUNKS + 4,)),
+        ],
+        compiler_params=pltpu.CompilerParams(
+            collective_id=0, has_side_effects=True, vmem_limit_bytes=56 * 2**20
+        ),
+        cost_estimate=pl.CostEstimate(
+            flops=2 * macs, bytes_accessed=2**23, transcendentals=8 * tok * half
+        ),
+    )(tokens[0], out_grad[0], dense, w_gate[0, 0], w_up[0, 0], w_down[0, 0])
+    tok_grad, out_g, out_u, out_d = outs
+    return (tok_grad[None], out_g[None, None], out_u[None, None], out_d[None, None])
+
+
 def solution(mesh):
     in_specs = (
         P("section", "expert", None),
@@ -140,6 +390,7 @@
         P("section", "expert", None, None),
         P("section", "expert", None, None),
     )
+    body = gathered if mesh.shape["expert"] == SLOTS else per_device
     return jax.shard_map(
-        per_device, mesh=mesh, in_specs=in_specs, out_specs=out_specs, check_vma=False
-    )
+        body, mesh=mesh, in_specs=in_specs, out_specs=out_specs, check_vma=False
+    )

time: 188 us -> 87.9 us (0.47)
  waiting for transfers between devices: 115 us -> 0 us
  Pallas kernels: 0 us -> 79.2 us
  starting transfers between devices: 21.3 us -> 0 us
  matrix products: 21.1 us -> 0 us
  local copies, waits for them, and re-layouts: 19.6 us -> 6.37 us
  other arithmetic: 9.22 us -> 0.01 us
    ppermute x6 -> x0, waiting for transfers between devices: 100 us -> none  [partner(): return lax.ppermute(value, axis, pairs)]
    pallas_call x0 -> x1, Pallas kernels: none -> 79.2 us  [gathered(): pl.pallas_call(functools.partial(gathered_kernel, sections, scale), out_s...]
    dot_general x8 -> x0, matrix products: 21.1 us -> none  [the longest x1 3.72 us: expert_grads(): gate_pre = jnp.dot(rows_in, gate_w, preferred_element_type=jnp.float32)]
    all_to_all x3 -> x0, waiting for transfers between devices: 15 us -> none  [the longest x1 15 us: per_device(): lax.all_to_all(slot_in, 'expert', split_axis=0, concat_axis=0, tiled=True)]
    all_to_all x3 -> x0, starting transfers between devices: 11.9 us -> none  [the longest x1 4.48 us: per_device(): lax.all_to_all(slot_in, 'expert', split_axis=0, concat_axis=0, tiled=True)]
    ppermute x6 -> x0, starting transfers between devices: 9.43 us -> none  [partner(): return lax.ppermute(value, axis, pairs)]
    gather x3 -> x0, local copies, waits for them, and re-layouts: 9.2 us -> none  [the longest x1 3.58 us: make_slots(): slot_grad = padded_grad[source].reshape(experts, cap, width)]
    broadcast_in_dim x3 -> x0, other arithmetic: 3.94 us -> none  [the longest x1 1.99 us: per_device(): out_d[None, None]]
  transfers between devices with their start and end apart: 9 -> 0, of which waited for: 7 -> 0; matrix products, arithmetic and copies ran while one was open for 17% -> 0% of each run, Pallas kernels for 0% -> 0%
where the time goes in v1:
time: 87.9 us; the launch traced here: 86.3 us
  Pallas kernels  79.2 us (90%)
  local copies, waits for them, and re-layouts  6.37 us (7%)
    pallas_call x1, Pallas kernels, gathered(): pl.pallas_call(functools.partial(gathered_kernel, sections, scale), out_s...  79.2 us
    unnamed x14, local copies, waits for them, and re-layouts  5.76 us

profile of v1, /device:TPU:0, one launch (start us, length us, event | category | flops | bytes accessed | tf_op | source)
XLA Modules:
  0.0 86.3 jit_solution(2356003774608341210)
XLA Ops:
  0.6 0.0 copy-start.4
  0.6 0.0 copy-start.3
  0.7 0.7 copy-done.4
  1.3 0.0 copy-done.3
  1.3 0.6 pad.4.gates_hbm
  1.9 79.2 %shard_map.102 = (bf16[192,1024]{1,0:T(8,128)(2,1)}, bf16[1024,256]{1,0:T(8,128)(2,1)}, bf16[1024,256]{1,0:T(8,128)(2,1)}, bf16[256,1024]{1,0:T(8,128)(2,1)}) custom-call(bf16[192,1024]{1,0:T(8,128)(2,1)} %bitcast.20, bf16[192,1024]{1,0:T(8,128)(2,1)} %bitcast.21, f32[8,256]{1,0:T(8,128)} %pad.4.gates_hbm, bf16[1024,256]{1,0:T(8,128)(2,1)} %bitcast.17, ...), custom_call_target="tpu_custom_call" | custom-call | flops 6442450944 | bytes 8388608 | tf_op jit(solution)/shard_map/pallas_call | solution.py:338
  81.2 0.0 copy-start.2
  81.2 1.8 %copy.17 = bf16[1,192,1024]{2,1,0:T(8,128)(2,1)} copy(bf16[1,192,1024]{2,1,0:T(8,128)(2,1)} %bitcast.14) | data formatting | bytes 786432
  83.0 0.0 copy-done.2
  83.0 0.0 copy-start.1
  83.0 0.8 copy.18
  83.8 0.4 copy-done.1
  84.2 0.0 copy-start
  84.2 0.8 copy.19
  85.0 0.4 copy-done
  85.5 0.8 copy.20
  (1 shorter events, 0.0 us)
Async XLA Ops:
  0.6 0.7 copy-start.4
  0.6 0.7 copy-start.3
  81.2 1.8 %copy-start.2 = (bf16[1024,256]{1,0:T(8,128)(2,1)S(1)}, bf16[1024,256]{1,0:T(8,128)(2,1)}, u32[]{:S(2)}) copy-start(bf16[1024,256]{1,0:T(8,128)(2,1)} %get-tuple-element.9) | copy-start | bytes 1572868
  83.0 1.2 %copy-start.1 = (bf16[1024,256]{1,0:T(8,128)(2,1)S(1)}, bf16[1024,256]{1,0:T(8,128)(2,1)}, u32[]{:S(2)}) copy-start(bf16[1024,256]{1,0:T(8,128)(2,1)} %get-tuple-element.10) | copy-start | bytes 1572868
  84.2 1.2 %copy-start = (bf16[256,1024]{1,0:T(8,128)(2,1)S(1)}, bf16[256,1024]{1,0:T(8,128)(2,1)}, u32[]{:S(2)}) copy-start(bf16[256,1024]{1,0:T(8,128)(2,1)} %get-tuple-element.11) | copy-start | bytes 1572868
